TPU v7x, 32 devices: a whole 2x2x4 slice. The times are simulated.
32 devices in a mesh: group: 2 (over x), fsdp: 2 (over core), tensor: 8 (over z, y).
Axes of the slice: x: 2, y: 2, z: 4, core: 2. Of those that a mesh axis runs over, the one named last changes fastest.
Arguments:
- row_states: bfloat16 [1024, 8192], P(('group', 'fsdp'), 'tensor'), parts along dimension 0, may hold values from -6 to 6
- norm_gain: float32 [8192], replicated, may hold values from 0.1 to 1.9
- exit_depth: int32 [1024], P(('group', 'fsdp')), parts along dimension 0, may hold values from 0 to 79
- gate_weight: bfloat16 [8192, 16384], P(None, ('fsdp', 'tensor')), may hold values from -0.0625 to 0.0625
- up_weight: bfloat16 [8192, 16384], P(None, ('fsdp', 'tensor')), may hold values from -0.0625 to 0.0625
- down_weight: bfloat16 [8192, 16384], P(None, ('fsdp', 'tensor')), may hold values from -0.0625 to 0.0625
- gate_delta: bfloat16 [8192, 16384], P(('fsdp', 'tensor')), may hold values from -4 to 4
- up_delta: bfloat16 [8192, 16384], P(('fsdp', 'tensor')), may hold values from -4 to 4
- down_delta: bfloat16 [8192, 16384], P(('fsdp', 'tensor')), may hold values from -4 to 4
- gate_index: int32 [128, 128], P(('fsdp', 'tensor')), may hold values from 0 to 255
- up_index: int32 [128, 128], P(('fsdp', 'tensor')), may hold values from 0 to 255
- down_index: int32 [128, 128], P(('fsdp', 'tensor')), may hold values from 0 to 255
- scale_table: float32 [256], replicated, may hold values from 0.002 to 0.01
Outputs:
- layer_out: bfloat16 [1024, 8192], P(('group', 'fsdp'), 'tensor'), parts along dimension 0
There are 2 independent parts, one for each index of `group`. A program takes and returns all parts, laid end to end along the dimension named above; an argument that names none is the same for every part. Nothing has to cross between parts.
All inputs are finite; a program needn't handle non-finite values.
Results may differ from a plain program's by a relative error of at most 0.0023.
The roundings to bfloat16 on the way count: a program that leaves them out, or rounds other values in their place, can miss the bound.
Values may be sent and summed in bfloat16 or wider, within the bound.
A program may use at most 448 MiB of HBM per device.

v0:
```python
import jax
import jax.numpy as jnp
from jax import lax
from jax.sharding import PartitionSpec as P

LAYER = 40


epsilon = 1e-05


def block_scales(index_values, scale_table):
    slots = index_values.astype(jnp.int32)
    entries = jnp.arange(scale_table.shape[0], dtype=jnp.int32)
    return jnp.sum(jnp.where(slots[..., None] == entries, scale_table, jnp.float32(0.0)), axis=-1)


def refresh(weight, delta, index_values, scale_table):
    block_count, col_blocks = index_values.shape
    total_rows, total_cols = weight.shape
    scales = block_scales(index_values, scale_table)
    shaped = delta.astype(jnp.float32).reshape(
        block_count, total_rows // block_count, col_blocks, total_cols // col_blocks
    )
    update = (shaped * scales[:, None, :, None]).reshape(total_rows, total_cols)
    return (weight.astype(jnp.float32) + update).astype(jnp.bfloat16)


def on_device(
    row_states,
    norm_gain,
    exit_depth,
    gate_weight,
    up_weight,
    down_weight,
    gate_delta,
    up_delta,
    down_delta,
    gate_index,
    up_index,
    down_index,
    scale_table,
):
    landed = (
        lax.all_to_all(gate_delta, ("fsdp", "tensor"), split_axis=1, concat_axis=0, tiled=True),
        lax.all_to_all(up_delta, ("fsdp", "tensor"), split_axis=1, concat_axis=0, tiled=True),
        lax.all_to_all(down_delta, ("fsdp", "tensor"), split_axis=1, concat_axis=0, tiled=True),
        lax.all_to_all(
            gate_index.astype(jnp.bfloat16),
            ("fsdp", "tensor"),
            split_axis=1,
            concat_axis=0,
            tiled=True,
        ),
        lax.all_to_all(
            up_index.astype(jnp.bfloat16),
            ("fsdp", "tensor"),
            split_axis=1,
            concat_axis=0,
            tiled=True,
        ),
        lax.all_to_all(
            down_index.astype(jnp.bfloat16),
            ("fsdp", "tensor"),
            split_axis=1,
            concat_axis=0,
            tiled=True,
        ),
    )
    fresh_gate = refresh(gate_weight, landed[0], landed[3], scale_table)
    fresh_up = refresh(up_weight, landed[1], landed[4], scale_table)
    fresh_down = refresh(down_weight, landed[2], landed[5], scale_table)
    full_rows = lax.all_gather(row_states, "tensor", axis=1, tiled=True)
    values = full_rows.astype(jnp.float32)
    mean_square = jnp.mean(values * values, axis=-1, keepdims=True)
    normed = (values * lax.rsqrt(mean_square + epsilon) * norm_gain).astype(jnp.bfloat16)
    piece_rows = lax.all_gather(normed, "fsdp", axis=0, tiled=True)
    gate_part = jnp.dot(piece_rows, fresh_gate, preferred_element_type=jnp.float32)
    up_part = jnp.dot(piece_rows, fresh_up, preferred_element_type=jnp.float32)
    hidden = (jax.nn.silu(gate_part) * up_part).astype(jnp.bfloat16)
    partial_sums = lax.dot_general(
        hidden, fresh_down, (((1,), (1,)), ((), ())), preferred_element_type=jnp.float32
    )
    feature_share = lax.psum_scatter(partial_sums, "tensor", scatter_dimension=1, tiled=True)
    summed = lax.psum_scatter(feature_share, "fsdp", scatter_dimension=0, tiled=True)
    active = (exit_depth > LAYER)[:, None]
    return (row_states.astype(jnp.float32) + jnp.where(active, summed, jnp.float32(0.0))).astype(
        jnp.bfloat16
    )


def solution(mesh):
    in_specs = (
        P(("group", "fsdp"), "tensor"),
        P(),
        P(("group", "fsdp")),
        P(None, ("fsdp", "tensor")),
        P(None, ("fsdp", "tensor")),
        P(None, ("fsdp", "tensor")),
        P(("fsdp", "tensor"), None),
        P(("fsdp", "tensor"), None),
        P(("fsdp", "tensor"), None),
        P(("fsdp", "tensor"), None),
        P(("fsdp", "tensor"), None),
        P(("fsdp", "tensor"), None),
        P(),
    )
    out_specs = P(("group", "fsdp"), "tensor")
    return jax.shard_map(
        on_device, mesh=mesh, in_specs=in_specs, out_specs=out_specs, check_vma=False
    )
```

profile of v0, /device:TPU:0, one launch (start us, length us, event | category | flops | bytes accessed | tf_op | source)
XLA Modules:
  0.0 1591.4 jit_solution(6983540541225021611)
XLA Ops:
  7.9 7.4 all-to-all-start.5
  35.4 22.4 %copy.50 = bf16[512,16384]{0,1:T(8,128)(2,1)} copy(bf16[512,16384]{1,0:T(8,128)(2,1)} %param.19) | data formatting | bytes 33554432 | tf_op args[6]
  57.7 21.7 %copy.51 = bf16[512,16,1024]{2,0,1:T(8,128)(2,1)} copy(bf16[512,16,1024]{0,2,1:T(8,128)(2,1)} %bitcast.60) | data formatting | bytes 33554432 | tf_op jit(solution)/shard_map/all_to_all | solution.py:45
  85.4 22.5 %copy.55 = bf16[512,16384]{0,1:T(8,128)(2,1)} copy(bf16[512,16384]{1,0:T(8,128)(2,1)} %param.20) | data formatting | bytes 33554432 | tf_op args[7]
  107.9 21.7 %copy.56 = bf16[512,16,1024]{2,0,1:T(8,128)(2,1)} copy(bf16[512,16,1024]{0,2,1:T(8,128)(2,1)} %bitcast.61) | data formatting | bytes 33554432 | tf_op jit(solution)/shard_map/all_to_all | solution.py:46
  129.5 298.5 %all-to-all-done = bf16[512,16,1024]{2,0,1:T(8,128)(2,1)} async-done(((bf16[512,16,1024]{2,0,1:T(8,128)(2,1)}), bf16[512,16,1024]{2,0,1:T(8,128)(2,1)}, u32[]{:S(2)}, u32[]{:S(2)}) %all-to-all-start) | async-done | bytes 16777248 | tf_op jit(solution)/shard_map/all_to_all | solution.py:45
  428.0 24.7 %all-to-all-start.2 = ((bf16[512,16,1024]{2,0,1:T(8,128)(2,1)}), bf16[512,16,1024]{2,0,1:T(8,128)(2,1)}, u32[]{:S(2)}, u32[]{:S(2)}) async-start(bf16[512,16,1024]{2,0,1:T(8,128)(2,1)} %copy.56), calls=%async_computation.2 | async-start | bytes 33554432 | tf_op jit(solution)/shard_map/all_to_all | solution.py:46
  452.7 22.4 %copy.60 = bf16[512,16384]{0,1:T(8,128)(2,1)} copy(bf16[512,16384]{1,0:T(8,128)(2,1)} %param.21) | data formatting | bytes 33554432 | tf_op args[8]
  475.1 21.7 %copy.61 = bf16[512,16,1024]{2,0,1:T(8,128)(2,1)} copy(bf16[512,16,1024]{0,2,1:T(8,128)(2,1)} %bitcast.62) | data formatting | bytes 33554432 | tf_op jit(solution)/shard_map/all_to_all | solution.py:47
  496.7 298.6 %all-to-all-done.2 = bf16[512,16,1024]{2,0,1:T(8,128)(2,1)} async-done(((bf16[512,16,1024]{2,0,1:T(8,128)(2,1)}), bf16[512,16,1024]{2,0,1:T(8,128)(2,1)}, u32[]{:S(2)}, u32[]{:S(2)}) %all-to-all-start.2) | async-done | bytes 16777248 | tf_op jit(solution)/shard_map/all_to_all | solution.py:46
  795.3 24.7 %all-to-all-start.4 = ((bf16[512,16,1024]{2,0,1:T(8,128)(2,1)}), bf16[512,16,1024]{2,0,1:T(8,128)(2,1)}, u32[]{:S(2)}, u32[]{:S(2)}) async-start(bf16[512,16,1024]{2,0,1:T(8,128)(2,1)} %copy.61), calls=%async_computation.4 | async-start | bytes 33554432 | tf_op jit(solution)/shard_map/all_to_all | solution.py:47
  820.8 162.1 %all-gather.3.cloned.1.call-done = bf16[256,8192]{1,0:T(8,128)(2,1)} async-done(((bf16[256,1024]{1,0:T(8,128)(2,1)}), bf16[256,8192]{1,0:T(8,128)(2,1)}) %all-gather.3.cloned.1.call-update) | async-done | bytes 4194320 | tf_op jit(solution)/shard_map/all_gather | solution.py:73
  992.9 11.1 mul.64
  1004.0 31.7 %fusion.5 = bf16[8192,1024]{1,0:T(8,128)(2,1)} fusion(f32[1024,8,8,128]{3,2,1,0:T(8,128)} %bitcast.57, bf16[8192,1024]{1,0:T(8,128)(2,1)} %param.16, bf16[512,16,1024]{2,0,1:T(8,128)(2,1)} %all-to-all-done), kind=kLoop, calls=%fused_computation.8 | loop fusion | flops 41943040 | bytes 83886080 | tf_op jit(solution)/shard_map/convert_element_type | solution.py:26
  1035.7 14.3 fusion.9
  1050.0 11.1 mul.68
  1061.1 29.0 %fusion.3 = bf16[8192,1024]{1,0:T(8,128)(2,1)} fusion(f32[1024,8,8,128]{3,2,1,0:T(8,128)} %bitcast.58, bf16[8192,1024]{1,0:T(8,128)(2,1)} %param.17, bf16[512,16,1024]{2,0,1:T(8,128)(2,1)} %all-to-all-done.2), kind=kLoop, calls=%fused_computation.5 | loop fusion | flops 41943040 | bytes 83886080 | tf_op jit(solution)/shard_map/convert_element_type | solution.py:26
  1090.1 14.9 multiply_convert_fusion
  1105.0 108.1 %all-to-all-done.4 = bf16[512,16,1024]{2,0,1:T(8,128)(2,1)} async-done(((bf16[512,16,1024]{2,0,1:T(8,128)(2,1)}), bf16[512,16,1024]{2,0,1:T(8,128)(2,1)}, u32[]{:S(2)}, u32[]{:S(2)}) %all-to-all-start.4) | async-done | bytes 16777248 | tf_op jit(solution)/shard_map/all_to_all | solution.py:47
  1213.1 11.1 mul.72
  1224.2 29.0 %fusion.1 = bf16[8192,1024]{1,0:T(8,128)(2,1)} fusion(f32[1024,8,8,128]{3,2,1,0:T(8,128)} %bitcast.59, bf16[8192,1024]{1,0:T(8,128)(2,1)} %param.18, bf16[512,16,1024]{2,0,1:T(8,128)(2,1)} %all-to-all-done.4), kind=kLoop, calls=%fused_computation.2 | loop fusion | flops 41943040 | bytes 83886080 | tf_op jit(solution)/shard_map/convert_element_type | solution.py:26
  1253.2 15.7 fusion.10
  1269.0 302.8 %reduce-scatter.3.cloned.1.call-done = f32[512,1024]{1,0:T(8,128)} async-done(((f32[512,8192]{1,0:T(8,128)}), f32[512,1024]{1,0:T(8,128)}) %reduce-scatter.3.cloned.1.call-update) | async-done | bytes 2097168 | tf_op jit(solution)/shard_map/reduce_scatter | solution.py:84
  1571.8 10.9 reduce-scatter.5.cloned.1.call-done
  (41 shorter events, 40.3 us)
Async XLA Ops:
  7.9 14.0 all-to-all-start.5
  21.9 10.0 all-to-all-start.3
  31.9 47.5 %all-to-all-start.1 = ((bf16[8,16,8]{2,0,1:T(8,128)(2,1)}), bf16[8,16,8]{2,0,1:T(8,128)(2,1)S(1)}, u32[]{:S(2)}, u32[]{:S(2)}) async-start(bf16[8,16,8]{2,0,1:T(8,128)(2,1)} %copy.52), calls=%async_computation.1 | async-start | bytes 65536 | tf_op jit(solution)/shard_map/all_to_all | solution.py:48
  79.4 348.6 %all-to-all-start = ((bf16[512,16,1024]{2,0,1:T(8,128)(2,1)}), bf16[512,16,1024]{2,0,1:T(8,128)(2,1)}, u32[]{:S(2)}, u32[]{:S(2)}) async-start(bf16[512,16,1024]{2,0,1:T(8,128)(2,1)} %copy.51), calls=%async_computation | async-start | bytes 33554432 | tf_op jit(solution)/shard_map/all_to_all | solution.py:45
  428.0 367.3 %all-to-all-start.2 = ((bf16[512,16,1024]{2,0,1:T(8,128)(2,1)}), bf16[512,16,1024]{2,0,1:T(8,128)(2,1)}, u32[]{:S(2)}, u32[]{:S(2)}) async-start(bf16[512,16,1024]{2,0,1:T(8,128)(2,1)} %copy.56), calls=%async_computation.2 | async-start | bytes 33554432 | tf_op jit(solution)/shard_map/all_to_all | solution.py:46
  496.7 489.3 %copy-start.1 = (f32[8192]{0:T(1024)S(1)}, f32[8192]{0:T(1024)}, u32[]{:S(2)}) copy-start(f32[8192]{0:T(1024)} %param.14) | copy-start | bytes 98308
  795.3 417.8 %all-to-all-start.4 = ((bf16[512,16,1024]{2,0,1:T(8,128)(2,1)}), bf16[512,16,1024]{2,0,1:T(8,128)(2,1)}, u32[]{:S(2)}, u32[]{:S(2)}) async-start(bf16[512,16,1024]{2,0,1:T(8,128)(2,1)} %copy.61), calls=%async_computation.4 | async-start | bytes 33554432 | tf_op jit(solution)/shard_map/all_to_all | solution.py:47
  820.0 171.7 %copy-start.2 = (f32[256]{0:T(256)S(1)}, f32[256]{0:T(256)}, u32[]{:S(2)}) copy-start(f32[256]{0:T(256)} %param.25) | copy-start | bytes 3076
  820.0 162.9 %all-gather.3.cloned.1.call-start = ((), (), s32[]{:S(2)}) async-start(), calls=%async_computation.8 | async-start | bytes 4718592 | tf_op jit(solution)/shard_map/all_gather | solution.py:73
  820.7 214.9 %all-gather.5.cloned.1.call-start = ((), (), s32[]{:S(2)}) async-start(), calls=%async_computation.9 | async-start | bytes 12582912 | tf_op jit(solution)/shard_map/all_gather | solution.py:77
  991.4 580.3 %reduce-scatter.3.cloned.1.call-start = ((), (), s32[]{:S(2)}) async-start(), calls=%async_computation.10 | async-start | bytes 18874368 | tf_op jit(solution)/shard_map/reduce_scatter | solution.py:84
  1268.9 302.9 %copy-start.3 = (s32[256]{0:T(256)S(1)}, s32[256]{0:T(256)}, u32[]{:S(2)}) copy-start(s32[256]{0:T(256)} %param.15) | copy-start | bytes 3076
  1268.9 313.8 %copy-start = (bf16[256,1024]{1,0:T(8,128)(2,1)S(1)}, bf16[256,1024]{1,0:T(8,128)(2,1)}, u32[]{:S(2)}) copy-start(bf16[256,1024]{1,0:T(8,128)(2,1)} %param.13) | copy-start | bytes 1572868
  1268.9 313.7 %reduce-scatter.5.cloned.1.call-start = ((), (), s32[]{:S(2)}) async-start(), calls=%async_computation.11 | async-start | bytes 3145728 | tf_op jit(solution)/shard_map/reduce_scatter | solution.py:85
Sparse Core Ops, SparseCore 0:
  823.0 159.8 all-gather.2
  991.5 34.3 all-gather.4
  1269.0 302.6 reduce-scatter.2
  1573.9 8.6 reduce-scatter.4
where the time goes:
time: 1600 us; the launch traced here: 1590 us
  waiting for transfers between devices  1190 us (74%)
  local copies, waits for them, and re-layouts  168 us (10%)
  other arithmetic  104 us (6%)
  starting transfers between devices  70.1 us (4%)
  matrix products  44.9 us (3%)
    reduce_scatter x1, waiting for transfers between devices, on_device(): lax.psum_scatter(partial_sums, 'tensor', scatter_dimension=1, tiled=True)  303 us
    all_to_all x1, waiting for transfers between devices, on_device(): lax.all_to_all(up_delta, ('fsdp', 'tensor'), split_axis=1, concat_axis=0,...  299 us
    all_to_all x1, waiting for transfers between devices, on_device(): lax.all_to_all(gate_delta, ('fsdp', 'tensor'), split_axis=1, concat_axis=...  298 us
    all_gather x1, waiting for transfers between devices, on_device(): full_rows = lax.all_gather(row_states, 'tensor', axis=1, tiled=True)  162 us
    all_to_all x1, waiting for transfers between devices, on_device(): lax.all_to_all(down_delta, ('fsdp', 'tensor'), split_axis=1, concat_axis=...  108 us
    convert_element_type x3, other arithmetic, refresh(): return (weight.astype(jnp.float32) + update).astype(jnp.bfloat16)  89.7 us
    unnamed x11, local copies, waits for them, and re-layouts  67.2 us
    mul x3, local copies, waits for them, and re-layouts, refresh(): update = (shaped * scales[:, None, :, None]).reshape(total_rows, total_cols)  33.3 us
  transfers between devices with their start and end apart: 10, of which 8 were waited for; matrix products, arithmetic and copies ran while one was open for 16% of the time, Pallas kernels for 0%

commit v1 on v0

v1 whole, which is shorter than its diff:
```python
import jax
import jax.numpy as jnp
from jax import lax
from jax.sharding import PartitionSpec as P

LAYER = 40
SHARDS = ("fsdp", "tensor")

epsilon = 1e-05


def block_scales(index_values, scale_table):
    entries = jnp.arange(scale_table.shape[0], dtype=jnp.int32)
    return jnp.sum(jnp.where(index_values[..., None] == entries, scale_table, jnp.float32(0.0)), axis=-1)


def land(delta, start, rows, shards):
    cols = delta.shape[1]
    part = lax.dynamic_slice_in_dim(delta, start, rows, axis=0)
    part = part.reshape(rows, shards, cols // shards).transpose(1, 0, 2)
    return lax.all_to_all(part, SHARDS, split_axis=0, concat_axis=0, tiled=True)


def refresh(weight, landed, scales):
    shards, rows, cols = landed.shape
    blocks, col_blocks = scales.shape[1:]
    shape = (shards, blocks, rows // blocks, col_blocks, cols // col_blocks)
    update = landed.astype(jnp.float32).reshape(shape) * scales[:, :, None, :, None]
    return (weight.astype(jnp.float32) + update.reshape(landed.shape)).astype(jnp.bfloat16)


def on_device(
    shards,
    groups,
    row_states,
    norm_gain,
    exit_depth,
    gate_weight,
    up_weight,
    down_weight,
    gate_delta,
    up_delta,
    down_delta,
    gate_index,
    up_index,
    down_index,
    scale_table,
):
    group = lax.axis_index("group")
    other = groups - 1 - group
    shard_rows = gate_delta.shape[0]
    half = shard_rows // groups
    cols = gate_weight.shape[1]
    block_rows = shard_rows // gate_index.shape[0]

    index = jnp.stack([gate_index, up_index, down_index], axis=1).astype(jnp.bfloat16)
    index = index.reshape(index.shape[0], 3, shards, -1).transpose(2, 1, 0, 3)
    index = lax.all_to_all(index, SHARDS, split_axis=0, concat_axis=0, tiled=True).astype(jnp.int32)
    scales = block_scales(index, scale_table)

    def swap(x):
        return lax.ppermute(x, "group", [(i, groups - 1 - i) for i in range(groups)])

    def fresh_part(weight, delta, which, offset, rows):
        start = group * half + offset
        landed = land(delta, start, rows, shards)
        view = weight.reshape(shards, shard_rows, cols)
        view = lax.dynamic_slice_in_dim(view, start, rows, axis=1)
        count = max(rows // block_rows, 1)
        part = lax.dynamic_slice_in_dim(scales[:, which], start // block_rows, count, axis=1)
        return refresh(view, landed, part)

    full_rows = lax.all_gather(row_states, "tensor", axis=1, tiled=True)
    values = full_rows.astype(jnp.float32)
    mean_square = jnp.mean(values * values, axis=-1, keepdims=True)
    normed = (values * lax.rsqrt(mean_square + epsilon) * norm_gain).astype(jnp.bfloat16)
    piece_rows = lax.all_gather(normed, "fsdp", axis=0, tiled=True)
    tokens = piece_rows.shape[0]
    split = piece_rows.reshape(tokens, shards, groups, half)

    def features(which):
        return lax.dynamic_index_in_dim(split, which, axis=2, keepdims=False).reshape(tokens, -1)

    mine_rows, other_rows = features(group), features(other)

    def project(weight, delta, which):
        mine = fresh_part(weight, delta, which, 0, half).reshape(-1, cols)
        theirs = swap(mine)
        return jnp.dot(mine_rows, mine, preferred_element_type=jnp.float32) + jnp.dot(
            other_rows, theirs, preferred_element_type=jnp.float32
        )

    gate_part = project(gate_weight, gate_delta, 0)
    up_part = project(up_weight, up_delta, 1)
    hidden = (jax.nn.silu(gate_part) * up_part).astype(jnp.bfloat16)

    def reduced(fresh):
        sums = lax.dot_general(
            hidden, fresh, (((1,), (1,)), ((), ())), preferred_element_type=jnp.float32
        )
        sums = lax.psum_scatter(sums, "fsdp", scatter_dimension=0, tiled=True)
        return lax.psum_scatter(sums, "tensor", scatter_dimension=1, tiled=True)

    pieces = 2
    rows = half // pieces
    own, far = [], []
    for piece in range(pieces):
        mine = fresh_part(down_weight, down_delta, 2, piece * rows, rows).reshape(-1, cols)
        theirs = swap(mine)
        own.append(reduced(mine))
        far.append(reduced(theirs))

    def joined(parts):
        return jnp.concatenate(
            [p.reshape(p.shape[0], -1, rows) for p in parts], axis=2
        )

    own, far = joined(own), joined(far)
    first = jnp.where(group == 0, own, far)
    second = jnp.where(group == 0, far, own)
    summed = jnp.stack([first, second], axis=2).reshape(row_states.shape)
    active = (exit_depth > LAYER)[:, None]
    return (row_states.astype(jnp.float32) + jnp.where(active, summed, jnp.float32(0.0))).astype(
        jnp.bfloat16
    )


def solution(mesh):
    shards = mesh.shape["fsdp"] * mesh.shape["tensor"]
    groups = mesh.shape["group"]

    def body(*arrays):
        return on_device(shards, groups, *arrays)

    in_specs = (
        P(("group", "fsdp"), "tensor"),
        P(),
        P(("group", "fsdp")),
        P(None, SHARDS),
        P(None, SHARDS),
        P(None, SHARDS),
        P(SHARDS, None),
        P(SHARDS, None),
        P(SHARDS, None),
        P(SHARDS, None),
        P(SHARDS, None),
        P(SHARDS, None),
        P(),
    )
    out_specs = P(("group", "fsdp"), "tensor")
    return jax.shard_map(body, mesh=mesh, in_specs=in_specs, out_specs=out_specs, check_vma=False)
```

time: 1600 us -> 1550 us (0.969)
  other arithmetic: 104 us -> 56 us
  local copies, waits for them, and re-layouts: 168 us -> 188 us
  waiting for transfers between devices: 1190 us -> 1170 us
    all_to_all x6 -> x5, waiting for transfers between devices: 715 us -> 253 us  [the longest x4 253 us: land(): return lax.all_to_all(part, SHARDS, split_axis=0, concat_axis=0, tiled=True)]
    ppermute x0 -> x4, waiting for transfers between devices: none -> 451 us  [swap(): lax.ppermute(x, 'group', [(i, groups - 1 - i) for i in range(groups)])]
    all_to_all x9 -> x0, local copies, waits for them, and re-layouts: 67.1 us -> none  [the longest x1 21.7 us: on_device(): lax.all_to_all(down_delta, ('fsdp', 'tensor'), split_axis=1, concat_axis=...]
    convert_element_type x9 -> x4, other arithmetic: 91.8 us -> 43.8 us  [the longest x3 43.8 us: refresh(): (weight.astype(jnp.float32) + update.reshape(landed.shape)).astype(jnp.bf...]
    mul x3 -> x10, local copies, waits for them, and re-layouts: 33.3 us -> 77.1 us  [refresh(): landed.astype(jnp.float32).reshape(shape) * scales[:, :, None, :, None]]
    reshape x0 -> x5, local copies, waits for them, and re-layouts: none -> 38.2 us  [the longest x4 37.4 us: land(): part = part.reshape(rows, shards, cols // shards).transpose(1, 0, 2)]
    unnamed x11 -> x27, local copies, waits for them, and re-layouts: 67.2 us -> 39.2 us
    dynamic_slice x0 -> x4, local copies, waits for them, and re-layouts: none -> 26.8 us  [the longest x3 22.7 us: land(): part = lax.dynamic_slice_in_dim(delta, start, rows, axis=0)]
  transfers between devices with their start and end apart: 10 -> 19, of which waited for: 8 -> 14; matrix products, arithmetic and copies ran while one was open for 16% -> 18% of each run, Pallas kernels for 0% -> 0%
where the time goes in v1:
time: 1550 us; the launch traced here: 1530 us
  waiting for transfers between devices  1170 us (75%)
  local copies, waits for them, and re-layouts  188 us (12%)
  other arithmetic  56 us (4%)
  starting transfers between devices  54.1 us (3%)
  matrix products  53.2 us (3%)
    ppermute x4, waiting for transfers between devices, swap(): lax.ppermute(x, 'group', [(i, groups - 1 - i) for i in range(groups)])  451 us
    reduce_scatter x4, waiting for transfers between devices, reduced(): return lax.psum_scatter(sums, 'tensor', scatter_dimension=1, tiled=True)  281 us
    all_to_all x4, waiting for transfers between devices, land(): return lax.all_to_all(part, SHARDS, split_axis=0, concat_axis=0, tiled=True)  253 us
    all_gather x1, waiting for transfers between devices, on_device(): full_rows = lax.all_gather(row_states, 'tensor', axis=1, tiled=True)  154 us
    mul x10, local copies, waits for them, and re-layouts, refresh(): landed.astype(jnp.float32).reshape(shape) * scales[:, :, None, :, None]  77.1 us
    convert_element_type x3, other arithmetic, refresh(): (weight.astype(jnp.float32) + update.reshape(landed.shape)).astype(jnp.bf...  43.8 us
    all_to_all x4, starting transfers between devices, land(): return lax.all_to_all(part, SHARDS, split_axis=0, concat_axis=0, tiled=True)  41.1 us
    unnamed x27, local copies, waits for them, and re-layouts  39.2 us
  transfers between devices with their start and end apart: 19, of which 14 were waited for; matrix products, arithmetic and copies ran while one was open for 18% of the time, Pallas kernels for 0%

profile of v1, /device:TPU:0, one launch (start us, length us, event | category | flops | bytes accessed | tf_op | source)
XLA Modules:
  0.0 1534.6 jit_solution(4937106577739407136)
XLA Ops:
  51.0 12.0 copy.55
  63.0 12.2 copy.46
  75.2 58.1 %all-to-all-done.3 = bf16[16,128,1024]{2,1,0:T(8,128)(2,1)} async-done(((bf16[16,128,1024]{2,1,0:T(8,128)(2,1)}), bf16[16,128,1024]{2,1,0:T(8,128)(2,1)}, u32[]{:S(2)}, u32[]{:S(2)}) %all-to-all-start.3) | async-done | bytes 4194336 | tf_op jit(solution)/shard_map/all_to_all | solution.py:21
  148.7 12.0 copy.56
  160.7 12.3 copy.49
  172.9 142.3 %all-to-all-done = bf16[16,256,1024]{2,1,0:T(8,128)(2,1)} async-done(((bf16[16,256,1024]{2,1,0:T(8,128)(2,1)}), bf16[16,256,1024]{2,1,0:T(8,128)(2,1)}, u32[]{:S(2)}, u32[]{:S(2)}) %all-to-all-start) | async-done | bytes 8388640 | tf_op jit(solution)/shard_map/all_to_all | solution.py:21
  315.2 13.6 all-to-all-start.2
  343.9 153.8 %all-gather.3.cloned.1.call-done = bf16[256,8192]{0,1:T(8,128)(2,1)} async-done(((bf16[256,1024]{0,1:T(8,128)(2,1)}), bf16[256,8192]{0,1:T(8,128)(2,1)}) %all-gather.3.cloned.1.call-update) | async-done | bytes 4194320 | tf_op jit(solution)/shard_map/all_gather | solution.py:73
  501.0 52.4 %all-to-all-done.2 = bf16[16,256,1024]{2,1,0:T(8,128)(2,1)} async-done(((bf16[16,256,1024]{2,1,0:T(8,128)(2,1)}), bf16[16,256,1024]{2,1,0:T(8,128)(2,1)}, u32[]{:S(2)}, u32[]{:S(2)}) %all-to-all-start.2) | async-done | bytes 8388640 | tf_op jit(solution)/shard_map/all_to_all | solution.py:21
  553.4 13.6 all-to-all-start.4
  578.4 18.9 %mul.92 = f32[16,256,1024]{2,1,0:T(8,128)} reshape(f32[16,4,64,8,128]{4,3,2,1,0:T(8,128)} %mul.91) | data formatting | bytes 33554432 | tf_op jit(solution)/shard_map/mul | solution.py:28
  604.2 18.0 %mul.97 = f32[16,256,1024]{2,1,0:T(8,128)} reshape(f32[16,4,64,8,128]{4,3,2,1,0:T(8,128)} %mul.96) | data formatting | bytes 33554432 | tf_op jit(solution)/shard_map/mul | solution.py:28
  622.2 15.8 %add_convert_fusion.1 = bf16[16,256,1024]{2,1,0:T(8,128)(2,1)} fusion(f32[16,256,1024]{2,1,0:T(8,128)} %mul.92, bf16[16,256,1024]{2,1,0:T(8,128)(2,1)} %all-to-all-done, bf16[16,512,1024]{2,1,0:T(8,128)(2,1)} %bitcast.69, s32[]{:T(128)S(6)} %select_n.73), kind=kLoop, calls=%fused_computation.1 | loop fusion | flops 20971520 | bytes 41943044 | tf_op jit(solution)/shard_map/convert_element_type | solution.py:29
  679.8 16.6 %add_convert_fusion.2 = (bf16[16,128,1024]{2,1,0:T(8,128)(2,1)}, bf16[16,128,1024]{2,1,0:T(8,128)(2,1)}) fusion(f32[16,128,1024]{2,1,0:T(8,128)} %mul.106, bf16[16,128,1024]{2,1,0:T(8,128)(2,1)} %all-to-all-done.4, bf16[16,512,1024]{2,1,0:T(8,128)(2,1)} %bitcast.71, s32[]{:T(128)S(6)} %select_n.78, f32[16,128,1024]{2,1,0:T(8,128)} %mul.102, ...), kind=kLoop, calls=%fused_computation.7 | loop fusion | flops 20971520 | bytes 41943048 | tf_op jit(solution)/shard_map/convert_element_type | solution.py:29
  715.1 106.6 %collective-permute-done = bf16[4096,1024]{1,0:T(8,128)(2,1)} collective-permute-done((bf16[4096,1024]{1,0:T(8,128)(2,1)}, bf16[4096,1024]{1,0:T(8,128)(2,1)}, u32[]{:S(2)}, u32[]{:S(2)}) %collective-permute-start) | collective-permute-done | bytes 8388640 | tf_op jit(solution)/shard_map/ppermute | solution.py:62
  828.8 172.6 %collective-permute-done.1 = bf16[4096,1024]{1,0:T(8,128)(2,1)} collective-permute-done((bf16[4096,1024]{1,0:T(8,128)(2,1)}, bf16[4096,1024]{1,0:T(8,128)(2,1)}, u32[]{:S(2)}, u32[]{:S(2)}) %collective-permute-start.1) | collective-permute-done | bytes 8388640 | tf_op jit(solution)/shard_map/ppermute | solution.py:62
  1009.6 81.2 %collective-permute-done.3 = bf16[2048,1024]{1,0:T(8,128)(2,1)} collective-permute-done((bf16[2048,1024]{1,0:T(8,128)(2,1)}, bf16[2048,1024]{1,0:T(8,128)(2,1)}, u32[]{:S(2)}, u32[]{:S(2)}) %collective-permute-start.3) | collective-permute-done | bytes 4194336 | tf_op jit(solution)/shard_map/ppermute | solution.py:62
  1098.8 90.8 %collective-permute-done.2 = bf16[2048,1024]{1,0:T(8,128)(2,1)S(1)} collective-permute-done((bf16[2048,1024]{1,0:T(8,128)(2,1)}, bf16[2048,1024]{1,0:T(8,128)(2,1)S(1)}, u32[]{:S(2)}, u32[]{:S(2)}) %collective-permute-start.2) | collective-permute-done | bytes 4194336 | tf_op jit(solution)/shard_map/ppermute | solution.py:62
  1209.2 13.3 reduce-scatter.9.cloned.1.call-done
  1222.6 15.5 %reduce-scatter.13.cloned.1.call-done = f32[256,2048]{1,0:T(8,128)} async-done(((f32[512,2048]{1,0:T(8,128)}), f32[256,2048]{1,0:T(8,128)}) %reduce-scatter.13.cloned.1.call-update) | async-done | bytes 2097168 | tf_op jit(solution)/shard_map/reduce_scatter | solution.py:101
  1238.1 72.9 %reduce-scatter.23.cloned.1.call-done = f32[256,256]{1,0:T(8,128)} async-done(((f32[256,2048]{1,0:T(8,128)}), f32[256,256]{1,0:T(8,128)}) %reduce-scatter.23.cloned.1.call-update) | async-done | bytes 262160 | tf_op jit(solution)/shard_map/reduce_scatter | solution.py:102
  1312.2 69.6 %reduce-scatter.19.cloned.1.call-done = f32[256,256]{1,0:T(8,128)} async-done(((f32[256,2048]{1,0:T(8,128)}), f32[256,256]{1,0:T(8,128)}) %reduce-scatter.19.cloned.1.call-update) | async-done | bytes 262160 | tf_op jit(solution)/shard_map/reduce_scatter | solution.py:102
  1382.9 69.6 %reduce-scatter.11.cloned.1.call-done = f32[256,256]{1,0:T(8,128)} async-done(((f32[256,2048]{1,0:T(8,128)}), f32[256,256]{1,0:T(8,128)}) %reduce-scatter.11.cloned.1.call-update) | async-done | bytes 262160 | tf_op jit(solution)/shard_map/reduce_scatter | solution.py:102
  1453.8 69.1 %reduce-scatter.15.cloned.1.call-done = f32[256,256]{1,0:T(8,128)} async-done(((f32[256,2048]{1,0:T(8,128)}), f32[256,256]{1,0:T(8,128)}) %reduce-scatter.15.cloned.1.call-update) | async-done | bytes 262160 | tf_op jit(solution)/shard_map/reduce_scatter | solution.py:102
  (107 shorter events, 207.4 us)
Async XLA Ops:
  9.6 27.8 %all-to-all-start.1 = ((bf16[16,3,8,8]{3,2,1,0:T(8,128)(2,1)}), bf16[16,3,8,8]{3,2,1,0:T(8,128)(2,1)S(1)}, u32[]{:S(2)}, u32[]{:S(2)}) async-start(bf16[16,3,8,8]{3,2,1,0:T(8,128)(2,1)} %copy.47), calls=%async_computation.1 | async-start | bytes 196608 | tf_op jit(solution)/shard_map/all_to_all | solution.py:58
  37.4 95.9 %all-to-all-start.3 = ((bf16[16,128,1024]{2,1,0:T(8,128)(2,1)}), bf16[16,128,1024]{2,1,0:T(8,128)(2,1)}, u32[]{:S(2)}, u32[]{:S(2)}) async-start(bf16[16,128,1024]{2,1,0:T(8,128)(2,1)} %bitcast.63), calls=%async_computation.3 | async-start | bytes 8388608 | tf_op jit(solution)/shard_map/all_to_all | solution.py:21
  133.3 181.9 %all-to-all-start = ((bf16[16,256,1024]{2,1,0:T(8,128)(2,1)}), bf16[16,256,1024]{2,1,0:T(8,128)(2,1)}, u32[]{:S(2)}, u32[]{:S(2)}) async-start(bf16[16,256,1024]{2,1,0:T(8,128)(2,1)} %bitcast.59), calls=%async_computation | async-start | bytes 16777216 | tf_op jit(solution)/shard_map/all_to_all | solution.py:21
  315.2 238.1 %all-to-all-start.2 = ((bf16[16,256,1024]{2,1,0:T(8,128)(2,1)}), bf16[16,256,1024]{2,1,0:T(8,128)(2,1)}, u32[]{:S(2)}, u32[]{:S(2)}) async-start(bf16[16,256,1024]{2,1,0:T(8,128)(2,1)} %bitcast.58), calls=%async_computation.2 | async-start | bytes 16777216 | tf_op jit(solution)/shard_map/all_to_all | solution.py:21
  328.8 168.9 %all-gather.3.cloned.1.call-start = ((), (), s32[]{:S(2)}) async-start(), calls=%async_computation.13 | async-start | bytes 4718592 | tf_op jit(solution)/shard_map/all_gather | solution.py:73
  553.4 126.4 %all-to-all-start.4 = ((bf16[16,128,1024]{2,1,0:T(8,128)(2,1)}), bf16[16,128,1024]{2,1,0:T(8,128)(2,1)}, u32[]{:S(2)}, u32[]{:S(2)}) async-start(bf16[16,128,1024]{2,1,0:T(8,128)(2,1)} %bitcast.62), calls=%async_computation.6 | async-start | bytes 8388608 | tf_op jit(solution)/shard_map/all_to_all | solution.py:21
  567.0 130.0 %all-gather.5.cloned.1.call-start = ((), (), s32[]{:S(2)}) async-start(), calls=%async_computation.14 | async-start | bytes 12582912 | tf_op jit(solution)/shard_map/all_gather | solution.py:77
  571.3 636.4 %reduce-scatter.21.cloned.1.call-start = ((), (), s32[]{:S(2)}) async-start(), calls=%async_computation.21 | async-start | bytes 6291456 | tf_op jit(solution)/shard_map/reduce_scatter | solution.py:101
  622.2 17.3 %slice-start.2 = ((s8[16777216]{0:T(1024)(128)(4,1)}), s8[4194304]{0:T(1024)(128)(4,1)S(1)}, s32[]{:S(2)}) async-start(s8[16777216]{0:T(1024)(128)(4,1)} %bitcast.56), calls=%async_computation.25 | async-start | bytes 8388608
  622.2 18.5 %slice-start.3 = ((s8[16777216]{0:T(1024)(128)(4,1)}), s8[4194304]{0:T(1024)(128)(4,1)S(1)}, s32[]{:S(2)}) async-start(s8[16777216]{0:T(1024)(128)(4,1)} %bitcast.56), calls=%async_computation.26 | async-start | bytes 8388608
  638.0 183.6 %collective-permute-start = (bf16[4096,1024]{1,0:T(8,128)(2,1)}, bf16[4096,1024]{1,0:T(8,128)(2,1)}, u32[]{:S(2)}, u32[]{:S(2)}) collective-permute-start(bf16[4096,1024]{1,0:T(8,128)(2,1)} %bitcast.7), channel_id=1, source_target_pairs={{0,16},{16,0},{1,17},{17,1},{2,18},{18,2},{3,19},{19,3},{4,20},{20... | collective-permute-start | bytes 25165832 | tf_op jit(solution)/shard_map/ppermute | solution.py:62
  652.0 349.4 %collective-permute-start.1 = (bf16[4096,1024]{1,0:T(8,128)(2,1)}, bf16[4096,1024]{1,0:T(8,128)(2,1)}, u32[]{:S(2)}, u32[]{:S(2)}) collective-permute-start(bf16[4096,1024]{1,0:T(8,128)(2,1)} %bitcast.13), channel_id=1, source_target_pairs={{0,16},{16,0},{1,17},{17,1},{2,18},{18,2},{3,19},{19,3},{4,20},{20... | collective-permute-start | bytes 25165832 | tf_op jit(solution)/shard_map/ppermute | solution.py:62
  696.4 394.3 %collective-permute-start.3 = (bf16[2048,1024]{1,0:T(8,128)(2,1)}, bf16[2048,1024]{1,0:T(8,128)(2,1)}, u32[]{:S(2)}, u32[]{:S(2)}) collective-permute-start(bf16[2048,1024]{1,0:T(8,128)(2,1)} %bitcast.22), channel_id=1, source_target_pairs={{0,16},{16,0},{1,17},{17,1},{2,18},{18,2},{3,19},{19,3},{4,20},{20... | collective-permute-start | bytes 12582920 | tf_op jit(solution)/shard_map/ppermute | solution.py:62
  1009.6 81.2 %copy-start.4 = (bf16[512,1024]{1,0:T(8,128)(2,1)}, bf16[512,1024]{1,0:T(8,128)(2,1)S(1)}, u32[]{:S(2)}) copy-start(bf16[512,1024]{1,0:T(8,128)(2,1)S(1)} %multiply_convert_fusion) | copy-start | bytes 3145732
  1097.3 92.4 %copy-start.5 = (bf16[512,1024]{1,0:T(8,128)(2,1)S(1)}, bf16[512,1024]{1,0:T(8,128)(2,1)}, u32[]{:S(2)}) copy-start(bf16[512,1024]{1,0:T(8,128)(2,1)} %copy-done.4) | copy-start | bytes 3145732
  1097.3 111.1 %reduce-scatter.17.cloned.1.call-start = ((), (), s32[]{:S(2)}) async-start(), calls=%async_computation.19 | async-start | bytes 6291456 | tf_op jit(solution)/shard_map/reduce_scatter | solution.py:101
  1097.3 92.3 %collective-permute-start.2 = (bf16[2048,1024]{1,0:T(8,128)(2,1)}, bf16[2048,1024]{1,0:T(8,128)(2,1)S(1)}, u32[]{:S(2)}, u32[]{:S(2)}) collective-permute-start(bf16[2048,1024]{1,0:T(8,128)(2,1)} %bitcast.67), channel_id=1, source_target_pairs={{0,16},{16,0},{1,17},{17,1},{2,18},{18,2},{3,19},{19,3},{4,20},{20... | collective-permute-start | bytes 12582920 | tf_op jit(solution)/shard_map/ppermute | solution.py:62
  1194.0 28.4 %reduce-scatter.9.cloned.1.call-start = ((), (), s32[]{:S(2)}) async-start(), calls=%async_computation.15 | async-start | bytes 6291456 | tf_op jit(solution)/shard_map/reduce_scatter | solution.py:101
  1200.7 37.4 %reduce-scatter.13.cloned.1.call-start = ((), (), s32[]{:S(2)}) async-start(), calls=%async_computation.17 | async-start | bytes 6291456 | tf_op jit(solution)/shard_map/reduce_scatter | solution.py:101
  1207.6 103.5 %reduce-scatter.23.cloned.1.call-start = ((), (), s32[]{:S(2)}) async-start(), calls=%async_computation.22 | async-start | bytes 2359296 | tf_op jit(solution)/shard_map/reduce_scatter | solution.py:102
  1207.7 30.4 %copy-start.3 = (s32[256]{0:T(256)S(1)}, s32[256]{0:T(256)}, u32[]{:S(2)}) copy-start(s32[256]{0:T(256)} %param.15) | copy-start | bytes 3076
  1208.4 173.4 %reduce-scatter.19.cloned.1.call-start = ((), (), s32[]{:S(2)}) async-start(), calls=%async_computation.20 | async-start | bytes 2359296 | tf_op jit(solution)/shard_map/reduce_scatter | solution.py:102
  1209.1 243.3 %reduce-scatter.11.cloned.1.call-start = ((), (), s32[]{:S(2)}) async-start(), calls=%async_computation.16 | async-start | bytes 2359296 | tf_op jit(solution)/shard_map/reduce_scatter | solution.py:102
  1222.5 300.4 %reduce-scatter.15.cloned.1.call-start = ((), (), s32[]{:S(2)}) async-start(), calls=%async_computation.18 | async-start | bytes 2359296 | tf_op jit(solution)/shard_map/reduce_scatter | solution.py:102
  (5 other events, 68.4 us)
Sparse Core Ops, SparseCore 0:
  331.8 165.8 all-gather.2
  571.4 19.5 all-gather.4
  1097.4 13.0 reduce-scatter.20
  1194.2 12.7 reduce-scatter.16
  1209.1 13.3 reduce-scatter.8
  1224.7 13.3 reduce-scatter.12
  1241.6 69.4 reduce-scatter.22
  1314.6 67.1 reduce-scatter.18
  1385.3 67.0 reduce-scatter.10
  1455.8 67.0 reduce-scatter.14

commit v2 on v1

v2 whole, which is shorter than its diff:
```python
import jax
import jax.numpy as jnp
from jax import lax
from jax.sharding import PartitionSpec as P

LAYER = 40
SHARDS = ("fsdp", "tensor")

epsilon = 1e-05


def block_scales(index_values, scale_table):
    entries = jnp.arange(scale_table.shape[0], dtype=jnp.int32)
    return jnp.sum(jnp.where(index_values[..., None] == entries, scale_table, jnp.float32(0.0)), axis=-1)


def after(x, *deps):
    return lax.optimization_barrier((x,) + deps)[0]


def cut(part, shards):
    rows, cols = part.shape
    return part.reshape(rows, shards, cols // shards).transpose(1, 0, 2)


def refresh(weight, landed, scales):
    shards, rows, cols = landed.shape
    blocks, col_blocks = scales.shape[1:]
    shape = (shards, blocks, rows // blocks, col_blocks, cols // col_blocks)
    update = landed.astype(jnp.float32).reshape(shape) * scales[:, :, None, :, None]
    return (weight.astype(jnp.float32) + update.reshape(landed.shape)).astype(jnp.bfloat16)


def on_device(
    tensor,
    shards,
    groups,
    row_states,
    norm_gain,
    exit_depth,
    gate_weight,
    up_weight,
    down_weight,
    gate_delta,
    up_delta,
    down_delta,
    gate_index,
    up_index,
    down_index,
    scale_table,
):
    group = lax.axis_index("group")
    other = groups - 1 - group
    shard_rows = gate_delta.shape[0]
    half = shard_rows // groups
    cols = gate_weight.shape[1]
    block_rows = shard_rows // gate_index.shape[0]

    index = jnp.stack([gate_index, up_index, down_index], axis=1).astype(jnp.bfloat16)
    index = index.reshape(index.shape[0], 3, shards, -1).transpose(2, 1, 0, 3)
    index = lax.all_to_all(index, SHARDS, split_axis=0, concat_axis=0, tiled=True).astype(jnp.int32)
    scales = block_scales(index, scale_table)

    def swap(x):
        return lax.ppermute(x, "group", [(i, groups - 1 - i) for i in range(groups)])

    full_rows = lax.all_gather(row_states, "tensor", axis=1, tiled=True)
    values = full_rows.astype(jnp.float32)
    mean_square = jnp.mean(values * values, axis=-1, keepdims=True)
    normed = (values * lax.rsqrt(mean_square + epsilon) * norm_gain).astype(jnp.bfloat16)
    piece_rows = lax.all_gather(normed, "fsdp", axis=0, tiled=True)
    tokens = piece_rows.shape[0]
    split = piece_rows.reshape(tokens, shards, groups, half)

    def features(which, offset, rows):
        part = lax.dynamic_index_in_dim(split, which, axis=2, keepdims=False)
        return part[:, :, offset : offset + rows].reshape(tokens, -1)

    small = half // 2
    jobs = [
        (gate_weight, gate_delta, 0, 0, small),
        (gate_weight, gate_delta, 0, small, small),
        (up_weight, up_delta, 1, 0, small),
        (up_weight, up_delta, 1, small, small),
        (down_weight, down_delta, 2, 0, small),
        (down_weight, down_delta, 2, small, small),
    ]
    own, far = [], []
    previous = None
    for number, (weight, delta, which, offset, rows) in enumerate(jobs):
        start = group * half + offset
        part = lax.dynamic_slice_in_dim(delta, start, rows, axis=0)
        if number == 0:
            part = after(part, full_rows)
        elif number == 1:
            part = after(part, previous)
        elif number == 2:
            part = after(part, own[0])
        else:
            part = after(part, own[number - 2], far[number - 3])
        previous = cut(part, shards)
        landed = lax.all_to_all(previous, SHARDS, split_axis=0, concat_axis=0, tiled=True)
        if number:
            landed = after(landed, own[number - 1])
        view = weight.reshape(shards, shard_rows, cols)
        view = lax.dynamic_slice_in_dim(view, start, rows, axis=1)
        count = max(rows // block_rows, 1)
        part = lax.dynamic_slice_in_dim(scales[:, which], start // block_rows, count, axis=1)
        mine = refresh(view, landed, part).reshape(-1, cols)
        own.append(mine)
        far.append(swap(mine))

    def project(which):
        total = jnp.float32(0.0)
        for where, held in ((group, own), (other, far)):
            for (_, _, place, offset, rows), fresh in zip(jobs, held):
                if place == which:
                    total = total + jnp.dot(
                        features(where, offset, rows), fresh, preferred_element_type=jnp.float32
                    )
        return total

    gate_part = project(0)
    up_part = project(1)
    hidden = (jax.nn.silu(gate_part) * up_part).astype(jnp.bfloat16)

    def reduced(hidden, parts):
        sums = [
            lax.dot_general(
                hidden, fresh, (((1,), (1,)), ((), ())), preferred_element_type=jnp.float32
            ).reshape(tokens, tensor, -1)
            for fresh in parts
        ]
        sums = jnp.concatenate(sums, axis=2).reshape(tokens, -1)
        sums = lax.psum_scatter(sums, "fsdp", scatter_dimension=0, tiled=True)
        sums = lax.psum_scatter(sums, "tensor", scatter_dimension=1, tiled=True)
        sums = sums.reshape(sums.shape[0], len(parts), -1, small)
        return sums.transpose(0, 2, 1, 3).reshape(sums.shape[0], -1, half)

    own_sums = reduced(hidden, own[4:])
    far_sums = reduced(after(hidden, own_sums), far[4:])
    first = jnp.where(group == 0, own_sums, far_sums)
    second = jnp.where(group == 0, far_sums, own_sums)
    summed = jnp.stack([first, second], axis=2).reshape(row_states.shape)
    active = (exit_depth > LAYER)[:, None]
    return (row_states.astype(jnp.float32) + jnp.where(active, summed, jnp.float32(0.0))).astype(
        jnp.bfloat16
    )


def solution(mesh):
    shards = mesh.shape["fsdp"] * mesh.shape["tensor"]
    groups = mesh.shape["group"]

    def body(*arrays):
        return on_device(mesh.shape["tensor"], shards, groups, *arrays)

    in_specs = (
        P(("group", "fsdp"), "tensor"),
        P(),
        P(("group", "fsdp")),
        P(None, SHARDS),
        P(None, SHARDS),
        P(None, SHARDS),
        P(SHARDS, None),
        P(SHARDS, None),
        P(SHARDS, None),
        P(SHARDS, None),
        P(SHARDS, None),
        P(SHARDS, None),
        P(),
    )
    out_specs = P(("group", "fsdp"), "tensor")
    return jax.shard_map(body, mesh=mesh, in_specs=in_specs, out_specs=out_specs, check_vma=False)
```

time: 1550 us -> 1220 us (0.79)
  waiting for transfers between devices: 1170 us -> 810 us
  other arithmetic: 56 us -> 84.5 us
    all_to_all x4 -> x6, waiting for transfers between devices: 253 us -> 140 us  [on_device(): lax.all_to_all(previous, SHARDS, split_axis=0, concat_axis=0, tiled=True)]
    reduce_scatter x4 -> x2, waiting for transfers between devices: 281 us -> 184 us  [reduced(): sums = lax.psum_scatter(sums, 'tensor', scatter_dimension=1, tiled=True)]
    all_gather x1, waiting for transfers between devices: 154 us -> 59.4 us  [on_device(): full_rows = lax.all_gather(row_states, 'tensor', axis=1, tiled=True)]
    ppermute x4 -> x6, waiting for transfers between devices: 451 us -> 409 us  [swap(): lax.ppermute(x, 'group', [(i, groups - 1 - i) for i in range(groups)])]
    unnamed x27 -> x37, local copies, waits for them, and re-layouts: 39.2 us -> 7.04 us
    dynamic_slice x4 -> x6, local copies, waits for them, and re-layouts: 26.8 us -> 45.5 us  [the longest x3 23.4 us: on_device(): part = lax.dynamic_slice_in_dim(delta, start, rows, axis=0)]
    convert_element_type x3 -> x6, other arithmetic: 43.8 us -> 60.4 us  [refresh(): (weight.astype(jnp.float32) + update.reshape(landed.shape)).astype(jnp.bf...]
    dot_general x4 -> x8, matrix products: 29.1 us -> 45 us  [project(): jnp.dot(features(where, offset, rows), fresh, preferred_element_type=jnp....]
  transfers between devices with their start and end apart: 19 -> 19, of which waited for: 14 -> 12; matrix products, arithmetic and copies ran while one was open for 18% -> 25% of each run, Pallas kernels for 0% -> 0%
where the time goes in v2:
time: 1220 us; the launch traced here: 1210 us
  waiting for transfers between devices  810 us (66%)
  local copies, waits for them, and re-layouts  185 us (15%)
  other arithmetic  84.5 us (7%)
  matrix products  58.6 us (5%)
  starting transfers between devices  54.5 us (4%)
  between operations  14.5 us (1%)
    ppermute x6, waiting for transfers between devices, swap(): lax.ppermute(x, 'group', [(i, groups - 1 - i) for i in range(groups)])  409 us
    reduce_scatter x2, waiting for transfers between devices, reduced(): sums = lax.psum_scatter(sums, 'tensor', scatter_dimension=1, tiled=True)  184 us
    all_to_all x6, waiting for transfers between devices, on_device(): lax.all_to_all(previous, SHARDS, split_axis=0, concat_axis=0, tiled=True)  140 us
    mul x14, local copies, waits for them, and re-layouts, refresh(): landed.astype(jnp.float32).reshape(shape) * scales[:, :, None, :, None]  79.1 us
    convert_element_type x6, other arithmetic, refresh(): (weight.astype(jnp.float32) + update.reshape(landed.shape)).astype(jnp.bf...  60.4 us
    all_gather x1, waiting for transfers between devices, on_device(): full_rows = lax.all_gather(row_states, 'tensor', axis=1, tiled=True)  59.4 us
    dot_general x8, matrix products, project(): jnp.dot(features(where, offset, rows), fresh, preferred_element_type=jnp....  45 us
    all_to_all x6, starting transfers between devices, on_device(): lax.all_to_all(previous, SHARDS, split_axis=0, concat_axis=0, tiled=True)  38.5 us
  transfers between devices with their start and end apart: 19, of which 12 were waited for; matrix products, arithmetic and copies ran while one was open for 25% of the time, Pallas kernels for 0%

profile of v2, /device:TPU:0, one launch (start us, length us, event | category | flops | bytes accessed | tf_op | source)
XLA Modules:
  0.0 1206.7 jit_solution(9650441543103498997)
XLA Ops:
  27.2 59.4 %all-gather.3.cloned.1.call-done = bf16[256,8192]{0,1:T(8,128)(2,1)} async-done(((bf16[256,1024]{0,1:T(8,128)(2,1)}), bf16[256,8192]{0,1:T(8,128)(2,1)}) %all-gather.3.cloned.1.call-update) | async-done | bytes 4194320 | tf_op jit(solution)/shard_map/all_gather | solution.py:67
  100.8 84.8 %all-to-all-done = bf16[16,128,1024]{2,1,0:T(8,128)(2,1)} async-done(((bf16[16,128,1024]{2,1,0:T(8,128)(2,1)}), bf16[16,128,1024]{2,1,0:T(8,128)(2,1)}, u32[]{:S(2)}, u32[]{:S(2)}) %all-to-all-start) | async-done | bytes 4194336 | tf_op jit(solution)/shard_map/all_to_all | solution.py:102
  206.3 9.3 mul.120
  215.7 10.4 add_convert_fusion.5
  228.5 54.8 %all-to-all-done.2 = bf16[16,128,1024]{2,1,0:T(8,128)(2,1)} async-done(((bf16[16,128,1024]{2,1,0:T(8,128)(2,1)}), bf16[16,128,1024]{2,1,0:T(8,128)(2,1)}, u32[]{:S(2)}, u32[]{:S(2)}) %all-to-all-start.2) | async-done | bytes 4194336 | tf_op jit(solution)/shard_map/all_to_all | solution.py:102
  296.9 9.3 mul.124
  306.2 10.4 add_convert_fusion.4
  316.6 68.2 %collective-permute-done = bf16[2048,1024]{1,0:T(8,128)(2,1)} collective-permute-done((bf16[2048,1024]{1,0:T(8,128)(2,1)}, bf16[2048,1024]{1,0:T(8,128)(2,1)}, u32[]{:S(2)}, u32[]{:S(2)}) %collective-permute-start) | collective-permute-done | bytes 4194336 | tf_op jit(solution)/shard_map/ppermute | solution.py:65
  412.6 9.3 mul.129
  428.1 10.5 add_convert_fusion.3
  438.6 47.9 %collective-permute-done.1 = bf16[2048,1024]{1,0:T(8,128)(2,1)} collective-permute-done((bf16[2048,1024]{1,0:T(8,128)(2,1)}, bf16[2048,1024]{1,0:T(8,128)(2,1)}, u32[]{:S(2)}, u32[]{:S(2)}) %collective-permute-start.1) | collective-permute-done | bytes 4194336 | tf_op jit(solution)/shard_map/ppermute | solution.py:65
  511.0 9.3 mul.133
  520.3 10.3 add_convert_fusion.2
  530.6 61.9 %collective-permute-done.2 = bf16[2048,1024]{1,0:T(8,128)(2,1)} collective-permute-done((bf16[2048,1024]{1,0:T(8,128)(2,1)}, bf16[2048,1024]{1,0:T(8,128)(2,1)}, u32[]{:S(2)}, u32[]{:S(2)}) %collective-permute-start.2) | collective-permute-done | bytes 4194336 | tf_op jit(solution)/shard_map/ppermute | solution.py:65
  621.8 9.3 mul.142
  691.1 10.4 add_convert_fusion.1
  701.6 55.0 %collective-permute-done.3 = bf16[2048,1024]{1,0:T(8,128)(2,1)} collective-permute-done((bf16[2048,1024]{1,0:T(8,128)(2,1)S(1)}, bf16[2048,1024]{1,0:T(8,128)(2,1)}, u32[]{:S(2)}, u32[]{:S(2)}) %collective-permute-start.3) | collective-permute-done | bytes 4194336 | tf_op jit(solution)/shard_map/ppermute | solution.py:65
  756.6 9.3 fusion.14
  793.8 91.7 %collective-permute-done.4 = bf16[2048,1024]{1,0:T(8,128)(2,1)S(1)} collective-permute-done((bf16[2048,1024]{1,0:T(8,128)(2,1)}, bf16[2048,1024]{1,0:T(8,128)(2,1)S(1)}, u32[]{:S(2)}, u32[]{:S(2)}) %collective-permute-start.4) | collective-permute-done | bytes 4194336 | tf_op jit(solution)/shard_map/ppermute | solution.py:65
  889.8 84.1 %collective-permute-done.5 = bf16[2048,1024]{1,0:T(8,128)(2,1)S(1)} collective-permute-done((bf16[2048,1024]{1,0:T(8,128)(2,1)}, bf16[2048,1024]{1,0:T(8,128)(2,1)S(1)}, u32[]{:S(2)}, u32[]{:S(2)}) %collective-permute-start.5) | collective-permute-done | bytes 4194336 | tf_op jit(solution)/shard_map/ppermute | solution.py:65
  982.8 9.9 copy.99
  993.5 17.0 %reduce-scatter.9.cloned.1.call-done = f32[256,4096]{0,1:T(8,128)} async-done(((f32[512,4096]{0,1:T(8,128)}), f32[256,4096]{0,1:T(8,128)}) %reduce-scatter.9.cloned.1.call-update) | async-done | bytes 4194320 | tf_op jit(solution)/shard_map/reduce_scatter | solution.py:135
  1010.6 92.8 %reduce-scatter.7.cloned.1.call-done = f32[256,512]{0,1:T(8,128)} async-done(((f32[256,4096]{0,1:T(8,128)}), f32[256,512]{0,1:T(8,128)}) %reduce-scatter.7.cloned.1.call-update) | async-done | bytes 524304 | tf_op jit(solution)/shard_map/reduce_scatter | solution.py:136
  1103.3 91.6 %reduce-scatter.11.cloned.1.call-done = f32[256,512]{0,1:T(8,128)} async-done(((f32[256,4096]{0,1:T(8,128)}), f32[256,512]{0,1:T(8,128)}) %reduce-scatter.11.cloned.1.call-update) | async-done | bytes 524304 | tf_op jit(solution)/shard_map/reduce_scatter | solution.py:136
  (128 shorter events, 265.1 us)
Async XLA Ops:
  6.5 80.1 %all-gather.3.cloned.1.call-start = ((), (), s32[]{:S(2)}) async-start(), calls=%async_computation.11 | async-start | bytes 4718592 | tf_op jit(solution)/shard_map/all_gather | solution.py:67
  11.7 79.7 %all-to-all-start.1 = ((bf16[16,3,8,8]{3,2,1,0:T(8,128)(2,1)}), bf16[16,3,8,8]{3,2,1,0:T(8,128)(2,1)S(1)}, u32[]{:S(2)}, u32[]{:S(2)}) async-start(bf16[16,3,8,8]{3,2,1,0:T(8,128)(2,1)} %copy.90), calls=%async_computation.1 | async-start | bytes 196608 | tf_op jit(solution)/shard_map/all_to_all | solution.py:61
  91.4 94.3 %all-to-all-start = ((bf16[16,128,1024]{2,1,0:T(8,128)(2,1)}), bf16[16,128,1024]{2,1,0:T(8,128)(2,1)}, u32[]{:S(2)}, u32[]{:S(2)}) async-start(bf16[16,128,1024]{2,1,0:T(8,128)(2,1)} %bitcast.152), calls=%async_computation | async-start | bytes 8388608 | tf_op jit(solution)/shard_map/all_to_all | solution.py:102
  185.7 97.7 %all-to-all-start.2 = ((bf16[16,128,1024]{2,1,0:T(8,128)(2,1)}), bf16[16,128,1024]{2,1,0:T(8,128)(2,1)}, u32[]{:S(2)}, u32[]{:S(2)}) async-start(bf16[16,128,1024]{2,1,0:T(8,128)(2,1)} %bitcast.145), calls=%async_computation.2 | async-start | bytes 8388608 | tf_op jit(solution)/shard_map/all_to_all | solution.py:102
  283.3 104.0 %all-to-all-start.3 = ((bf16[16,128,1024]{2,1,0:T(8,128)(2,1)}), bf16[16,128,1024]{2,1,0:T(8,128)(2,1)}, u32[]{:S(2)}, u32[]{:S(2)}) async-start(bf16[16,128,1024]{2,1,0:T(8,128)(2,1)} %bitcast.150), calls=%async_computation.3 | async-start | bytes 8388608 | tf_op jit(solution)/shard_map/all_to_all | solution.py:102
  291.5 93.4 %collective-permute-start = (bf16[2048,1024]{1,0:T(8,128)(2,1)}, bf16[2048,1024]{1,0:T(8,128)(2,1)}, u32[]{:S(2)}, u32[]{:S(2)}) collective-permute-start(bf16[2048,1024]{1,0:T(8,128)(2,1)} %bitcast.173), channel_id=1, source_target_pairs={{0,16},{16,0},{1,17},{17,1},{2,18},{18,2},{3,19},{19,3},{4,20},{20... | collective-permute-start | bytes 12582920 | tf_op jit(solution)/shard_map/ppermute | solution.py:65
  306.2 78.7 %copy-start.2 = (bf16[128,16384]{1,0:T(8,128)(2,1)S(1)}, bf16[128,16384]{1,0:T(8,128)(2,1)}, u32[]{:S(2)}) copy-start(bf16[128,16384]{1,0:T(8,128)(2,1)} %get-tuple-element.21) | copy-start | bytes 12582916
  387.4 105.5 %all-to-all-start.4 = ((bf16[16,128,1024]{2,1,0:T(8,128)(2,1)}), bf16[16,128,1024]{2,1,0:T(8,128)(2,1)}, u32[]{:S(2)}, u32[]{:S(2)}) async-start(bf16[16,128,1024]{2,1,0:T(8,128)(2,1)} %bitcast.147), calls=%async_computation.4 | async-start | bytes 8388608 | tf_op jit(solution)/shard_map/all_to_all | solution.py:102
  393.2 237.9 %all-gather.5.cloned.1.call-start = ((), (), s32[]{:S(2)}) async-start(), calls=%async_computation.12 | async-start | bytes 12582912 | tf_op jit(solution)/shard_map/all_gather | solution.py:71
  393.2 93.2 %collective-permute-start.1 = (bf16[2048,1024]{1,0:T(8,128)(2,1)}, bf16[2048,1024]{1,0:T(8,128)(2,1)}, u32[]{:S(2)}, u32[]{:S(2)}) collective-permute-start(bf16[2048,1024]{1,0:T(8,128)(2,1)} %bitcast.174), channel_id=1, source_target_pairs={{0,16},{16,0},{1,17},{17,1},{2,18},{18,2},{3,19},{19,3},{4,20},{20... | collective-permute-start | bytes 12582920 | tf_op jit(solution)/shard_map/ppermute | solution.py:65
  412.6 12.8 %copy-start.12 = (f32[8192]{0:T(1024)S(1)}, f32[8192]{0:T(1024)}, u32[]{:S(2)}) copy-start(f32[8192]{0:T(1024)} %param.14) | copy-start | bytes 98308
  492.8 106.1 %all-to-all-start.5 = ((bf16[16,128,1024]{2,1,0:T(8,128)(2,1)}), bf16[16,128,1024]{2,1,0:T(8,128)(2,1)}, u32[]{:S(2)}, u32[]{:S(2)}) async-start(bf16[16,128,1024]{2,1,0:T(8,128)(2,1)} %bitcast.149), calls=%async_computation.5 | async-start | bytes 8388608 | tf_op jit(solution)/shard_map/all_to_all | solution.py:102
  499.2 93.4 %collective-permute-start.2 = (bf16[2048,1024]{1,0:T(8,128)(2,1)}, bf16[2048,1024]{1,0:T(8,128)(2,1)}, u32[]{:S(2)}, u32[]{:S(2)}) collective-permute-start(bf16[2048,1024]{1,0:T(8,128)(2,1)} %bitcast.175), channel_id=1, source_target_pairs={{0,16},{16,0},{1,17},{17,1},{2,18},{18,2},{3,19},{19,3},{4,20},{20... | collective-permute-start | bytes 12582920 | tf_op jit(solution)/shard_map/ppermute | solution.py:65
  598.9 172.4 %all-to-all-start.6 = ((bf16[16,128,1024]{2,1,0:T(8,128)(2,1)}), bf16[16,128,1024]{2,1,0:T(8,128)(2,1)}, u32[]{:S(2)}, u32[]{:S(2)}) async-start(bf16[16,128,1024]{2,1,0:T(8,128)(2,1)} %bitcast.146), calls=%async_computation.6 | async-start | bytes 8388608 | tf_op jit(solution)/shard_map/all_to_all | solution.py:102
  604.7 388.1 %reduce-scatter.5.cloned.1.call-start = ((), (), s32[]{:S(2)}) async-start(), calls=%async_computation.13 | async-start | bytes 12582912 | tf_op jit(solution)/shard_map/reduce_scatter | solution.py:135
  663.7 92.9 %collective-permute-start.3 = (bf16[2048,1024]{1,0:T(8,128)(2,1)S(1)}, bf16[2048,1024]{1,0:T(8,128)(2,1)}, u32[]{:S(2)}, u32[]{:S(2)}) collective-permute-start(bf16[2048,1024]{1,0:T(8,128)(2,1)S(1)} %bitcast.176), channel_id=1, source_target_pairs={{0,16},{16,0},{1,17},{17,1},{2,18},{18,2},{3,19},{19,3},{4,20},{20... | collective-permute-start | bytes 12582920 | tf_op jit(solution)/shard_map/ppermute | solution.py:65
  701.6 65.3 %copy-start.8 = (bf16[16,128,1024]{2,1,0:T(8,128)(2,1)S(1)}, bf16[16,128,1024]{2,1,0:T(8,128)(2,1)}, u32[]{:S(2)}) copy-start(bf16[16,128,1024]{2,1,0:T(8,128)(2,1)} %add_convert_fusion.1) | copy-start | bytes 12582916
  791.6 218.9 %reduce-scatter.9.cloned.1.call-start = ((), (), s32[]{:S(2)}) async-start(), calls=%async_computation.15 | async-start | bytes 12582912 | tf_op jit(solution)/shard_map/reduce_scatter | solution.py:135
  791.7 93.8 %collective-permute-start.4 = (bf16[2048,1024]{1,0:T(8,128)(2,1)}, bf16[2048,1024]{1,0:T(8,128)(2,1)S(1)}, u32[]{:S(2)}, u32[]{:S(2)}) collective-permute-start(bf16[2048,1024]{1,0:T(8,128)(2,1)} %bitcast.177), channel_id=1, source_target_pairs={{0,16},{16,0},{1,17},{17,1},{2,18},{18,2},{3,19},{19,3},{4,20},{20... | collective-permute-start | bytes 12582920 | tf_op jit(solution)/shard_map/ppermute | solution.py:65
  793.2 180.6 %collective-permute-start.5 = (bf16[2048,1024]{1,0:T(8,128)(2,1)}, bf16[2048,1024]{1,0:T(8,128)(2,1)S(1)}, u32[]{:S(2)}, u32[]{:S(2)}) collective-permute-start(bf16[2048,1024]{1,0:T(8,128)(2,1)} %bitcast.180), channel_id=1, source_target_pairs={{0,16},{16,0},{1,17},{17,1},{2,18},{18,2},{3,19},{19,3},{4,20},{20... | collective-permute-start | bytes 12582920 | tf_op jit(solution)/shard_map/ppermute | solution.py:65
  992.7 110.6 %reduce-scatter.7.cloned.1.call-start = ((), (), s32[]{:S(2)}) async-start(), calls=%async_computation.14 | async-start | bytes 4718592 | tf_op jit(solution)/shard_map/reduce_scatter | solution.py:136
  992.8 17.7 %copy-start.14 = (s32[256]{0:T(256)S(1)}, s32[256]{0:T(256)}, u32[]{:S(2)}) copy-start(s32[256]{0:T(256)} %param.15) | copy-start | bytes 3076
  993.3 201.6 %reduce-scatter.11.cloned.1.call-start = ((), (), s32[]{:S(2)}) async-start(), calls=%async_computation.16 | async-start | bytes 4718592 | tf_op jit(solution)/shard_map/reduce_scatter | solution.py:136
  1010.6 188.1 %copy-start.11 = (bf16[256,1024]{1,0:T(8,128)(2,1)S(1)}, bf16[256,1024]{1,0:T(8,128)(2,1)}, u32[]{:S(2)}) copy-start(bf16[256,1024]{1,0:T(8,128)(2,1)} %param.13) | copy-start | bytes 1572868
  (12 other events, 68.5 us)
Sparse Core Ops, SparseCore 0:
  9.5 77.0 all-gather.2
  428.2 18.6 all-gather.4
  791.7 17.8 reduce-scatter.4
  992.8 17.6 reduce-scatter.8
  1014.0 89.3 reduce-scatter.6
  1107.3 87.6 reduce-scatter.10

commit v3 on v2

--- a/solution.py
+++ b/solution.py
@@ -138,7 +138,8 @@
         return sums.transpose(0, 2, 1, 3).reshape(sums.shape[0], -1, half)
 
     own_sums = reduced(hidden, own[4:])
-    far_sums = reduced(after(hidden, own_sums), far[4:])
+    held, own_sums = lax.optimization_barrier((far[4:], own_sums))
+    far_sums = reduced(hidden, held)
     first = jnp.where(group == 0, own_sums, far_sums)
     second = jnp.where(group == 0, far_sums, own_sums)
     summed = jnp.stack([first, second], axis=2).reshape(row_states.shape)

time: 1220 us -> 1160 us (0.951)
  waiting for transfers between devices: 810 us -> 741 us
    ppermute x6, waiting for transfers between devices: 409 us -> 321 us  [swap(): lax.ppermute(x, 'group', [(i, groups - 1 - i) for i in range(groups)])]
    reduce_scatter x2, waiting for transfers between devices: 17 us -> 36 us  [reduced(): sums = lax.psum_scatter(sums, 'fsdp', scatter_dimension=0, tiled=True)]
    unnamed x37 -> x38, local copies, waits for them, and re-layouts: 7.04 us -> 20.7 us
  transfers between devices with their start and end apart: 19 -> 19, of which waited for: 12 -> 12; matrix products, arithmetic and copies ran while one was open for 25% -> 24% of each run, Pallas kernels for 0% -> 0%
where the time goes in v3:
time: 1160 us; the launch traced here: 1150 us
  waiting for transfers between devices  741 us (64%)
  local copies, waits for them, and re-layouts  193 us (17%)
  other arithmetic  82.6 us (7%)
  matrix products  62.9 us (5%)
  starting transfers between devices  54.1 us (5%)
  between operations  14.3 us (1%)
    ppermute x6, waiting for transfers between devices, swap(): lax.ppermute(x, 'group', [(i, groups - 1 - i) for i in range(groups)])  321 us
    reduce_scatter x2, waiting for transfers between devices, reduced(): sums = lax.psum_scatter(sums, 'tensor', scatter_dimension=1, tiled=True)  185 us
    all_to_all x6, waiting for transfers between devices, on_device(): lax.all_to_all(previous, SHARDS, split_axis=0, concat_axis=0, tiled=True)  140 us
    mul x14, local copies, waits for them, and re-layouts, refresh(): landed.astype(jnp.float32).reshape(shape) * scales[:, :, None, :, None]  79.1 us
    convert_element_type x6, other arithmetic, refresh(): (weight.astype(jnp.float32) + update.reshape(landed.shape)).astype(jnp.bf...  60.7 us
    all_gather x1, waiting for transfers between devices, on_device(): full_rows = lax.all_gather(row_states, 'tensor', axis=1, tiled=True)  59.4 us
    dot_general x8, matrix products, project(): jnp.dot(features(where, offset, rows), fresh, preferred_element_type=jnp....  45 us
    all_to_all x6, starting transfers between devices, on_device(): lax.all_to_all(previous, SHARDS, split_axis=0, concat_axis=0, tiled=True)  38.3 us
  transfers between devices with their start and end apart: 19, of which 12 were waited for; matrix products, arithmetic and copies ran while one was open for 24% of the time, Pallas kernels for 0%

profile of v3, /device:TPU:0, one launch (start us, length us, event | category | flops | bytes accessed | tf_op | source)
XLA Modules:
  0.0 1147.6 jit_solution(9534450401402947702)
XLA Ops:
  27.2 59.4 %all-gather.3.cloned.1.call-done = bf16[256,8192]{0,1:T(8,128)(2,1)} async-done(((bf16[256,1024]{0,1:T(8,128)(2,1)}), bf16[256,8192]{0,1:T(8,128)(2,1)}) %all-gather.3.cloned.1.call-update) | async-done | bytes 4194320 | tf_op jit(solution)/shard_map/all_gather | solution.py:67
  100.8 84.8 %all-to-all-done = bf16[16,128,1024]{2,1,0:T(8,128)(2,1)} async-done(((bf16[16,128,1024]{2,1,0:T(8,128)(2,1)}), bf16[16,128,1024]{2,1,0:T(8,128)(2,1)}, u32[]{:S(2)}, u32[]{:S(2)}) %all-to-all-start) | async-done | bytes 4194336 | tf_op jit(solution)/shard_map/all_to_all | solution.py:102
  206.3 9.3 mul.115
  215.7 10.4 add_convert_fusion.5
  228.5 54.8 %all-to-all-done.3 = bf16[16,128,1024]{2,1,0:T(8,128)(2,1)} async-done(((bf16[16,128,1024]{2,1,0:T(8,128)(2,1)}), bf16[16,128,1024]{2,1,0:T(8,128)(2,1)}, u32[]{:S(2)}, u32[]{:S(2)}) %all-to-all-start.3) | async-done | bytes 4194336 | tf_op jit(solution)/shard_map/all_to_all | solution.py:102
  297.1 9.3 mul.119
  306.4 10.4 add_convert_fusion.4
  316.8 68.2 %collective-permute-done.1 = bf16[2048,1024]{1,0:T(8,128)(2,1)} collective-permute-done((bf16[2048,1024]{1,0:T(8,128)(2,1)}, bf16[2048,1024]{1,0:T(8,128)(2,1)}, u32[]{:S(2)}, u32[]{:S(2)}) %collective-permute-start.1) | collective-permute-done | bytes 4194336 | tf_op jit(solution)/shard_map/ppermute | solution.py:65
  412.9 9.3 mul.123
  428.3 10.5 add_convert_fusion.3
  438.8 47.8 %collective-permute-done = bf16[2048,1024]{1,0:T(8,128)(2,1)} collective-permute-done((bf16[2048,1024]{1,0:T(8,128)(2,1)}, bf16[2048,1024]{1,0:T(8,128)(2,1)}, u32[]{:S(2)}, u32[]{:S(2)}) %collective-permute-start) | collective-permute-done | bytes 4194336 | tf_op jit(solution)/shard_map/ppermute | solution.py:65
  510.8 9.3 mul.127
  520.1 10.3 add_convert_fusion.2
  530.4 61.9 %collective-permute-done.3 = bf16[2048,1024]{1,0:T(8,128)(2,1)} collective-permute-done((bf16[2048,1024]{1,0:T(8,128)(2,1)}, bf16[2048,1024]{1,0:T(8,128)(2,1)}, u32[]{:S(2)}, u32[]{:S(2)}) %collective-permute-start.3) | collective-permute-done | bytes 4194336 | tf_op jit(solution)/shard_map/ppermute | solution.py:65
  621.6 9.3 mul.135
  691.0 10.7 add_convert_fusion.1
  701.7 54.8 %collective-permute-done.5 = bf16[2048,1024]{1,0:T(8,128)(2,1)} collective-permute-done((bf16[2048,1024]{1,0:T(8,128)(2,1)S(1)}, bf16[2048,1024]{1,0:T(8,128)(2,1)}, u32[]{:S(2)}, u32[]{:S(2)}) %collective-permute-start.5) | collective-permute-done | bytes 4194336 | tf_op jit(solution)/shard_map/ppermute | solution.py:65
  756.5 9.3 fusion.14
  791.3 18.0 %reduce-scatter.5.cloned.1.call-done = f32[256,4096]{0,1:T(8,128)} async-done(((f32[512,4096]{0,1:T(8,128)}), f32[256,4096]{0,1:T(8,128)}) %reduce-scatter.5.cloned.1.call-update) | async-done | bytes 4194320 | tf_op jit(solution)/shard_map/reduce_scatter | solution.py:135
  811.4 90.9 %reduce-scatter.7.cloned.1.call-done = f32[256,512]{0,1:T(8,128)} async-done(((f32[256,4096]{0,1:T(8,128)}), f32[256,512]{0,1:T(8,128)}) %reduce-scatter.7.cloned.1.call-update) | async-done | bytes 524304 | tf_op jit(solution)/shard_map/reduce_scatter | solution.py:136
  904.4 88.0 %collective-permute-done.4 = bf16[2048,1024]{1,0:T(8,128)(2,1)} collective-permute-done((bf16[2048,1024]{1,0:T(8,128)(2,1)}, bf16[2048,1024]{1,0:T(8,128)(2,1)}, u32[]{:S(2)}, u32[]{:S(2)}) %collective-permute-start.4) | collective-permute-done | bytes 4194336 | tf_op jit(solution)/shard_map/ppermute | solution.py:65
  1010.7 11.6 %copy.112 = f32[64,8,8,512]{3,1,2,0:T(8,128)} copy(f32[64,8,8,512]{3,2,1,0:T(8,128)S(1)} %bitcast.146) | data formatting | bytes 16777216
  1022.4 18.1 %reduce-scatter.9.cloned.1.call-done = f32[256,4096]{1,0:T(8,128)} async-done(((f32[512,4096]{1,0:T(8,128)}), f32[256,4096]{1,0:T(8,128)}) %reduce-scatter.9.cloned.1.call-update) | async-done | bytes 4194320 | tf_op jit(solution)/shard_map/reduce_scatter | solution.py:135
  1040.5 93.6 %reduce-scatter.11.cloned.1.call-done = f32[256,512]{1,0:T(8,128)} async-done(((f32[256,4096]{1,0:T(8,128)}), f32[256,512]{1,0:T(8,128)}) %reduce-scatter.11.cloned.1.call-update) | async-done | bytes 524304 | tf_op jit(solution)/shard_map/reduce_scatter | solution.py:136
  (133 shorter events, 273.0 us)
Async XLA Ops:
  6.5 80.1 %all-gather.3.cloned.1.call-start = ((), (), s32[]{:S(2)}) async-start(), calls=%async_computation.11 | async-start | bytes 4718592 | tf_op jit(solution)/shard_map/all_gather | solution.py:67
  11.7 79.7 %all-to-all-start.1 = ((bf16[16,3,8,8]{3,2,1,0:T(8,128)(2,1)}), bf16[16,3,8,8]{3,2,1,0:T(8,128)(2,1)S(1)}, u32[]{:S(2)}, u32[]{:S(2)}) async-start(bf16[16,3,8,8]{3,2,1,0:T(8,128)(2,1)} %copy.90), calls=%async_computation.1 | async-start | bytes 196608 | tf_op jit(solution)/shard_map/all_to_all | solution.py:61
  91.4 94.3 %all-to-all-start = ((bf16[16,128,1024]{2,1,0:T(8,128)(2,1)}), bf16[16,128,1024]{2,1,0:T(8,128)(2,1)}, u32[]{:S(2)}, u32[]{:S(2)}) async-start(bf16[16,128,1024]{2,1,0:T(8,128)(2,1)} %bitcast.153), calls=%async_computation | async-start | bytes 8388608 | tf_op jit(solution)/shard_map/all_to_all | solution.py:102
  185.7 97.7 %all-to-all-start.3 = ((bf16[16,128,1024]{2,1,0:T(8,128)(2,1)}), bf16[16,128,1024]{2,1,0:T(8,128)(2,1)}, u32[]{:S(2)}, u32[]{:S(2)}) async-start(bf16[16,128,1024]{2,1,0:T(8,128)(2,1)} %bitcast.147), calls=%async_computation.3 | async-start | bytes 8388608 | tf_op jit(solution)/shard_map/all_to_all | solution.py:102
  215.7 10.4 copy-start.3
  283.3 104.2 %all-to-all-start.2 = ((bf16[16,128,1024]{2,1,0:T(8,128)(2,1)}), bf16[16,128,1024]{2,1,0:T(8,128)(2,1)}, u32[]{:S(2)}, u32[]{:S(2)}) async-start(bf16[16,128,1024]{2,1,0:T(8,128)(2,1)} %bitcast.152), calls=%async_computation.2 | async-start | bytes 8388608 | tf_op jit(solution)/shard_map/all_to_all | solution.py:102
  291.7 93.4 %collective-permute-start.1 = (bf16[2048,1024]{1,0:T(8,128)(2,1)}, bf16[2048,1024]{1,0:T(8,128)(2,1)}, u32[]{:S(2)}, u32[]{:S(2)}) collective-permute-start(bf16[2048,1024]{1,0:T(8,128)(2,1)} %bitcast.175), channel_id=1, source_target_pairs={{0,16},{16,0},{1,17},{17,1},{2,18},{18,2},{3,19},{19,3},{4,20},{20... | collective-permute-start | bytes 12582920 | tf_op jit(solution)/shard_map/ppermute | solution.py:65
  306.4 78.7 %copy-start.2 = (bf16[128,16384]{1,0:T(8,128)(2,1)S(1)}, bf16[128,16384]{1,0:T(8,128)(2,1)}, u32[]{:S(2)}) copy-start(bf16[128,16384]{1,0:T(8,128)(2,1)} %get-tuple-element.25) | copy-start | bytes 12582916
  387.5 105.5 %all-to-all-start.5 = ((bf16[16,128,1024]{2,1,0:T(8,128)(2,1)}), bf16[16,128,1024]{2,1,0:T(8,128)(2,1)}, u32[]{:S(2)}, u32[]{:S(2)}) async-start(bf16[16,128,1024]{2,1,0:T(8,128)(2,1)} %bitcast.149), calls=%async_computation.5 | async-start | bytes 8388608 | tf_op jit(solution)/shard_map/all_to_all | solution.py:102
  393.3 237.6 %all-gather.5.cloned.1.call-start = ((), (), s32[]{:S(2)}) async-start(), calls=%async_computation.12 | async-start | bytes 12582912 | tf_op jit(solution)/shard_map/all_gather | solution.py:71
  393.4 93.2 %collective-permute-start = (bf16[2048,1024]{1,0:T(8,128)(2,1)}, bf16[2048,1024]{1,0:T(8,128)(2,1)}, u32[]{:S(2)}, u32[]{:S(2)}) collective-permute-start(bf16[2048,1024]{1,0:T(8,128)(2,1)} %bitcast.176), channel_id=1, source_target_pairs={{0,16},{16,0},{1,17},{17,1},{2,18},{18,2},{3,19},{19,3},{4,20},{20... | collective-permute-start | bytes 12582920 | tf_op jit(solution)/shard_map/ppermute | solution.py:65
  412.9 12.8 %copy-start.12 = (f32[8192]{0:T(1024)S(1)}, f32[8192]{0:T(1024)}, u32[]{:S(2)}) copy-start(f32[8192]{0:T(1024)} %param.14) | copy-start | bytes 98308
  493.0 105.7 %all-to-all-start.4 = ((bf16[16,128,1024]{2,1,0:T(8,128)(2,1)}), bf16[16,128,1024]{2,1,0:T(8,128)(2,1)}, u32[]{:S(2)}, u32[]{:S(2)}) async-start(bf16[16,128,1024]{2,1,0:T(8,128)(2,1)} %bitcast.151), calls=%async_computation.4 | async-start | bytes 8388608 | tf_op jit(solution)/shard_map/all_to_all | solution.py:102
  499.0 93.4 %collective-permute-start.3 = (bf16[2048,1024]{1,0:T(8,128)(2,1)}, bf16[2048,1024]{1,0:T(8,128)(2,1)}, u32[]{:S(2)}, u32[]{:S(2)}) collective-permute-start(bf16[2048,1024]{1,0:T(8,128)(2,1)} %bitcast.177), channel_id=1, source_target_pairs={{0,16},{16,0},{1,17},{17,1},{2,18},{18,2},{3,19},{19,3},{4,20},{20... | collective-permute-start | bytes 12582920 | tf_op jit(solution)/shard_map/ppermute | solution.py:65
  598.8 172.4 %all-to-all-start.6 = ((bf16[16,128,1024]{2,1,0:T(8,128)(2,1)}), bf16[16,128,1024]{2,1,0:T(8,128)(2,1)}, u32[]{:S(2)}, u32[]{:S(2)}) async-start(bf16[16,128,1024]{2,1,0:T(8,128)(2,1)} %bitcast.148), calls=%async_computation.6 | async-start | bytes 8388608 | tf_op jit(solution)/shard_map/all_to_all | solution.py:102
  604.6 204.7 %reduce-scatter.5.cloned.1.call-start = ((), (), s32[]{:S(2)}) async-start(), calls=%async_computation.13 | async-start | bytes 12582912 | tf_op jit(solution)/shard_map/reduce_scatter | solution.py:135
  663.6 92.9 %collective-permute-start.5 = (bf16[2048,1024]{1,0:T(8,128)(2,1)S(1)}, bf16[2048,1024]{1,0:T(8,128)(2,1)}, u32[]{:S(2)}, u32[]{:S(2)}) collective-permute-start(bf16[2048,1024]{1,0:T(8,128)(2,1)S(1)} %bitcast.178), channel_id=1, source_target_pairs={{0,16},{16,0},{1,17},{17,1},{2,18},{18,2},{3,19},{19,3},{4,20},{20... | collective-permute-start | bytes 12582920 | tf_op jit(solution)/shard_map/ppermute | solution.py:65
  701.7 65.1 %copy-start.8 = (bf16[16,128,1024]{2,1,0:T(8,128)(2,1)S(1)}, bf16[16,128,1024]{2,1,0:T(8,128)(2,1)}, u32[]{:S(2)}) copy-start(bf16[16,128,1024]{2,1,0:T(8,128)(2,1)} %add_convert_fusion.1) | copy-start | bytes 12582916
  791.3 111.1 %reduce-scatter.7.cloned.1.call-start = ((), (), s32[]{:S(2)}) async-start(), calls=%async_computation.14 | async-start | bytes 4718592 | tf_op jit(solution)/shard_map/reduce_scatter | solution.py:136
  809.3 231.2 %reduce-scatter.9.cloned.1.call-start = ((), (), s32[]{:S(2)}) async-start(), calls=%async_computation.15 | async-start | bytes 12582912 | tf_op jit(solution)/shard_map/reduce_scatter | solution.py:135
  809.3 95.0 %collective-permute-start.2 = (bf16[2048,1024]{1,0:T(8,128)(2,1)}, bf16[2048,1024]{1,0:T(8,128)(2,1)}, u32[]{:S(2)}, u32[]{:S(2)}) collective-permute-start(bf16[2048,1024]{1,0:T(8,128)(2,1)} %bitcast.179), channel_id=1, source_target_pairs={{0,16},{16,0},{1,17},{17,1},{2,18},{18,2},{3,19},{19,3},{4,20},{20... | collective-permute-start | bytes 12582920 | tf_op jit(solution)/shard_map/ppermute | solution.py:65
  811.2 181.2 %collective-permute-start.4 = (bf16[2048,1024]{1,0:T(8,128)(2,1)}, bf16[2048,1024]{1,0:T(8,128)(2,1)}, u32[]{:S(2)}, u32[]{:S(2)}) collective-permute-start(bf16[2048,1024]{1,0:T(8,128)(2,1)} %bitcast.182), channel_id=1, source_target_pairs={{0,16},{16,0},{1,17},{17,1},{2,18},{18,2},{3,19},{19,3},{4,20},{20... | collective-permute-start | bytes 12582920 | tf_op jit(solution)/shard_map/ppermute | solution.py:65
  1022.4 18.1 %copy-start.14 = (s32[256]{0:T(256)S(1)}, s32[256]{0:T(256)}, u32[]{:S(2)}) copy-start(s32[256]{0:T(256)} %param.15) | copy-start | bytes 3076
  1022.4 111.8 %reduce-scatter.11.cloned.1.call-start = ((), (), s32[]{:S(2)}) async-start(), calls=%async_computation.16 | async-start | bytes 4718592 | tf_op jit(solution)/shard_map/reduce_scatter | solution.py:136
  (12 other events, 61.1 us)
Sparse Core Ops, SparseCore 0:
  9.5 77.0 all-gather.2
  428.4 18.6 all-gather.4
  791.4 17.8 reduce-scatter.4
  813.2 89.1 reduce-scatter.6
  1022.5 17.9 reduce-scatter.8
  1044.4 89.6 reduce-scatter.10
